TPU v7x, 256 devices: a whole 4x4x8 slice. The times are simulated.
256 devices in a mesh: gx: 16 (over y_hi, z), gy: 4 (over y_lo, core), gz: 4 (over x).
Axes of the slice: x: 4, y: 4 (y_hi: 2, y_lo: 2; y = y_hi * 2 + y_lo), z: 8, core: 2. Of those that a mesh axis runs over, the one named last changes fastest.
Arguments:
- snapshot: bfloat16 [32, 16, 128, 512], P(None, 'gx', 'gy', 'gz'), may hold values from -6 to 6
- snap_index: int32 [1], replicated, may hold values from 0 to 63
- snap_means: float32 [64, 32], replicated, may hold values from -0.5 to 0.5
- snap_scales: float32 [64, 32], replicated, may hold values from 0.5 to 2
- out_bias: float32 [32], replicated, may hold values from -3 to 3
- kernel: bfloat16 [32, 32, 3, 3, 3], replicated, may hold values from -0.21875 to 0.21875
- cotangent: bfloat16 [32, 16, 128, 512], P(None, 'gx', 'gy', 'gz'), may hold values from -6 to 6
Outputs:
- predicted: bfloat16 [32, 16, 128, 512], P(None, 'gx', 'gy', 'gz')
- snapshot_grad: bfloat16 [32, 16, 128, 512], P(None, 'gx', 'gy', 'gz')
- kernel_grad: float32 [32, 32, 3, 3, 3], replicated
- bias_grad: float32 [32], replicated
All inputs are finite; a program needn't handle non-finite values.
Results may differ from a plain program's by a relative error of at most 0.0046.
Values may be sent and summed in bfloat16 or wider, within the bound.
A program may use at most 64 MiB of HBM per device.

v0:
```python
import math

import jax
import jax.numpy as jnp
from jax import lax
from jax.sharding import PartitionSpec as P


def extended(cells, sides, width):
    for axis, dim in sides:
        count = lax.axis_size(axis)
        head = lax.slice_in_dim(cells, 0, width, axis=dim)
        tail = lax.slice_in_dim(cells, cells.shape[dim] - width, cells.shape[dim], axis=dim)
        cells = jnp.concatenate(
            [
                lax.ppermute(tail, axis, [(i, (i + 1) % count) for i in range(count)]),
                cells,
                lax.ppermute(head, axis, [((i + 1) % count, i) for i in range(count)]),
            ],
            axis=dim,
        )
    return cells


def select_row(table, snap_index):
    stored = table.shape[0]
    one_hot = (jnp.arange(stored, dtype=jnp.int32)[:, None] == snap_index[0]).astype(table.dtype)
    return jnp.sum(one_hot * table, 0)


def window(padded_field, step_x, step_y, extent_x, extent_y, extent_z, flipped):
    slabs = []
    for step_z in range(3):
        if flipped:
            start_x, start_y, start_z = (2 - step_x, 2 - step_y, 2 - step_z)
        else:
            start_x, start_y, start_z = (step_x, step_y, step_z)
        slabs.append(
            padded_field[
                :,
                start_x : start_x + extent_x,
                start_y : start_y + extent_y,
                start_z : start_z + extent_z,
            ]
        )
    return jnp.stack(slabs, 1)


def body(snapshot, snap_index, snap_means, snap_scales, out_bias, kernel, cotangent):
    centre = select_row(snap_means, snap_index)[:, None, None, None]
    spread = (1.0 / select_row(snap_scales, snap_index))[:, None, None, None]
    normed = ((snapshot.astype(jnp.float32) - centre) * spread).astype(jnp.bfloat16)
    channels, extent_x, extent_y, extent_z = normed.shape
    stacked = jnp.stack([normed, cotangent])
    padded = extended(stacked, (("gx", 2), ("gy", 3), ("gz", 4)), 1)
    wall_rows = lax.broadcasted_iota(jnp.int32, (1, 1, 1, extent_y + 2, 1), 3)
    wall_index = lax.axis_index("gy")
    wall_count = lax.axis_size("gy")
    outside = (wall_rows == 0) & (wall_index == 0) | (wall_rows == extent_y + 1) & (
        wall_index == wall_count - 1
    )
    padded = jnp.where(outside, jnp.zeros((), jnp.bfloat16), padded)
    halo_field = padded[0]
    halo_grad = padded[1]
    whole_cells = (
        extent_x
        * lax.axis_size("gx")
        * extent_y
        * lax.axis_size("gy")
        * extent_z
        * lax.axis_size("gz")
    )
    factor = 1.0 / math.sqrt(whole_cells)
    output_sum = jnp.zeros((channels, extent_x, extent_y, extent_z), jnp.float32)
    input_sum = jnp.zeros((channels, extent_x, extent_y, extent_z), jnp.float32)
    bias_local = jnp.sum(cotangent.astype(jnp.float32), (1, 2, 3))
    for step_x in range(3):
        for step_y in range(3):
            slabs = window(halo_field, step_x, step_y, extent_x, extent_y, extent_z, False)
            output_sum = output_sum + jnp.einsum(
                "ock,ckxyz->oxyz",
                kernel[:, :, step_x, step_y, :],
                slabs,
                preferred_element_type=jnp.float32,
            )
    for step_x in range(3):
        for step_y in range(3):
            grad_slabs = window(halo_grad, step_x, step_y, extent_x, extent_y, extent_z, True)
            input_sum = input_sum + jnp.einsum(
                "ock,okxyz->cxyz",
                kernel[:, :, step_x, step_y, :],
                grad_slabs,
                preferred_element_type=jnp.float32,
            )
    pieces = []
    for step_x in range(3):
        for step_y in range(3):
            kernel_slabs = window(halo_field, step_x, step_y, extent_x, extent_y, extent_z, False)
            pieces.append(
                jnp.einsum(
                    "oxyz,ckxyz->ock", cotangent, kernel_slabs, preferred_element_type=jnp.float32
                )
            )
    kernel_total, bias_total = lax.psum(
        (jnp.stack(pieces, 2).reshape(channels, channels, 3, 3, 3), bias_local), ("gx", "gy", "gz")
    )
    predicted = (output_sum + out_bias[:, None, None, None]).astype(jnp.bfloat16)
    snapshot_grad = (input_sum * spread).astype(jnp.bfloat16)
    return (predicted, snapshot_grad, kernel_total * factor, bias_total * factor)


def solution(mesh):
    in_specs = (P(None, "gx", "gy", "gz"), P(), P(), P(), P(), P(), P(None, "gx", "gy", "gz"))
    out_specs = (P(None, "gx", "gy", "gz"), P(None, "gx", "gy", "gz"), P(), P())
    return jax.shard_map(body, mesh=mesh, in_specs=in_specs, out_specs=out_specs, check_vma=False)
```

profile of v0, /device:TPU:1, one launch (start us, length us, event | category | flops | bytes accessed | tf_op | source)
XLA Modules:
  0.0 409.0 jit_solution(1824700474075007514)
XLA Ops:
  9.8 1.2 fusion.67
  11.1 9.1 %collective-permute-start.1 = (bf16[2,32,1,32,128]{4,1,3,2,0:T(8,128)(2,1)S(1)}, bf16[2,32,1,32,128]{4,1,3,2,0:T(8,128)(2,1)S(1)}, u32[]{:S(2)}, u32[]{:S(2)}) collective-permute-start(bf16[2,32,1,32,128]{4,1,3,2,0:T(8,128)(2,1)S(1)} %pad_maximum_fusion.1), channel_id=1, source_target_pairs={{16,0},{32,16},{48,32},{64,48},{80,64},{96,80},{112,96},{128,112},... | collective-permute-start | bytes 1572872 | tf_op jit(solution)/shard_map/ppermute | solution.py:18
  20.5 82.2 %psum.15 = f32[32]{0:T(128)S(1)} all-reduce(f32[32]{0:T(128)S(1)} %convert_reduce_fusion), channel_id=1, replica_groups=mesh['gx'=16,'gy'=4,'gz'=4] {'gx','gy','gz'}, use_global_device_ids=true, to_apply=%region_4.5 | all-reduce | flops 32 | bytes 256 | tf_op jit(solution)/shard_map/psum | solution.py:104
  102.8 1.5 collective-permute-start.2
  105.5 2.3 collective-permute-done.3
  108.9 2.2 copy.56
  111.1 2.2 copy.57
  113.3 1.5 collective-permute-start.5
  114.8 4.1 %collective-permute-done.4 = bf16[2,32,3,34,1]{3,1,4,2,0:T(8,128)(2,1)S(1)} collective-permute-done((bf16[2,32,3,34,1]{3,1,4,2,0:T(8,128)(2,1)S(1)}, bf16[2,32,3,34,1]{3,1,4,2,0:T(8,128)(2,1)S(1)}, u32[]{:S(2)}, u32[]{:S(2)}) %collective-permute-start.4) | collective-permute-done | bytes 13088 | tf_op jit(solution)/shard_map/ppermute | solution.py:16
  119.0 3.0 copy.58
  122.0 3.0 copy.59
  125.0 5.7 %maximum_select_fusion = bf16[2,32,3,34,130]{4,1,3,2,0:T(8,128)(2,1)S(1)} fusion(bf16[2,32,3,34,1]{4,1,3,2,0:T(8,128)(2,1)S(1)} %copy.59, bf16[2,32,3,1,128]{4,1,3,2,0:T(8,128)(2,1)S(1)} %collective-permute-done.3, bf16[2,32,1,32,128]{4,1,3,2,0:T(8,128)(2,1)} %copy-done.2, bf16[1,32,1,32,128]{4,1,3,2,0:T(8,128)(2,1)} %bitcast.492, ...), kind=kLoop, calls=%fused_computation | loop fusion | flops 14426880 | bytes 3394594 | tf_op jit(solution)/shard_map/jit(_where)/select_n | solution.py:62
  132.7 1.7 slice_bitcast_fusion.27
  134.4 3.0 slice_bitcast_fusion.28
  142.2 1.9 convolution_bitcast_fusion.4
  144.4 1.8 convolution_bitcast_fusion.3
  146.6 1.8 convolution_bitcast_fusion.2
  148.8 1.9 convolution_bitcast_fusion.1
  151.0 1.8 convolution_bitcast_fusion
  154.0 2.0 copy.98
  156.0 1.5 convolution_bitcast_fusion.15
  165.6 1.3 fusion.21
  169.7 230.6 %all-reduce.2.cloned.1.call-done = f32[32,32,3,3,3]{1,0,4,3,2:T(8,128)} async-done(((f32[32,32,3,3,3]{1,0,4,3,2:T(8,128)}), f32[32,32,3,3,3]{1,0,4,3,2:T(8,128)}) %all-reduce.2.cloned.1.call-update) | async-done | bytes 110608 | tf_op jit(solution)/shard_map/psum | solution.py:104
  400.3 1.8 broadcast_multiply_fusion
  (111 shorter events, 24.4 us)
Async XLA Ops:
  7.2 13.1 %copy-start.4 = (bf16[32,1,32,128]{3,2,1,0:T(8,128)(2,1)S(1)}, bf16[32,1,32,128]{3,2,1,0:T(8,128)(2,1)}, u32[]{:S(2)}) copy-start(bf16[32,1,32,128]{3,2,1,0:T(8,128)(2,1)} %param.13) | copy-start | bytes 786436
  7.2 393.1 %all-reduce.2.cloned.1.call-start = ((), (), s32[]{:S(2)}) async-start(), calls=%async_computation | async-start | bytes 884736 | tf_op jit(solution)/shard_map/psum | solution.py:104
  9.8 98.0 %copy-start = (bf16[32,1,32,128]{3,0,2,1:T(8,128)(2,1)}, bf16[32,1,32,128]{3,0,2,1:T(8,128)(2,1)S(1)}, u32[]{:S(2)}) copy-start(bf16[32,1,32,128]{3,0,2,1:T(8,128)(2,1)S(1)} %copy.202) | copy-start | bytes 786436
  11.0 96.8 %copy-start.1 = (bf16[1,32,1,32,128]{4,1,3,2,0:T(8,128)(2,1)}, bf16[1,32,1,32,128]{4,1,3,2,0:T(8,128)(2,1)S(1)}, u32[]{:S(2)}) copy-start(bf16[1,32,1,32,128]{4,1,3,2,0:T(8,128)(2,1)S(1)} %fusion.67) | copy-start | bytes 786436
  11.1 91.7 %collective-permute-start.1 = (bf16[2,32,1,32,128]{4,1,3,2,0:T(8,128)(2,1)S(1)}, bf16[2,32,1,32,128]{4,1,3,2,0:T(8,128)(2,1)S(1)}, u32[]{:S(2)}, u32[]{:S(2)}) collective-permute-start(bf16[2,32,1,32,128]{4,1,3,2,0:T(8,128)(2,1)S(1)} %pad_maximum_fusion.1), channel_id=1, source_target_pairs={{16,0},{32,16},{48,32},{64,48},{80,64},{96,80},{112,96},{128,112},... | collective-permute-start | bytes 1572872 | tf_op jit(solution)/shard_map/ppermute | solution.py:18
  20.2 82.6 %collective-permute-start = (bf16[2,32,1,32,128]{4,1,3,2,0:T(8,128)(2,1)S(1)}, bf16[2,32,1,32,128]{4,1,3,2,0:T(8,128)(2,1)S(1)}, u32[]{:S(2)}, u32[]{:S(2)}) collective-permute-start(bf16[2,32,1,32,128]{4,1,3,2,0:T(8,128)(2,1)S(1)} %pad_maximum_fusion.1), channel_id=1, source_target_pairs={{0,16},{16,32},{32,48},{48,64},{64,80},{80,96},{96,112},{112,128},... | collective-permute-start | bytes 1572872 | tf_op jit(solution)/shard_map/ppermute | solution.py:16
  102.8 5.0 %copy-start.2 = (bf16[2,32,1,32,128]{4,1,3,2,0:T(8,128)(2,1)}, bf16[2,32,1,32,128]{4,1,3,2,0:T(8,128)(2,1)S(1)}, u32[]{:S(2)}) copy-start(bf16[2,32,1,32,128]{4,1,3,2,0:T(8,128)(2,1)S(1)} %collective-permute-done.1) | copy-start | bytes 1572868
  102.8 5.0 %copy-start.3 = (bf16[2,32,1,32,128]{4,1,3,2,0:T(8,128)(2,1)}, bf16[2,32,1,32,128]{4,1,3,2,0:T(8,128)(2,1)S(1)}, u32[]{:S(2)}) copy-start(bf16[2,32,1,32,128]{4,1,3,2,0:T(8,128)(2,1)S(1)} %collective-permute-done) | copy-start | bytes 1572868
  102.8 2.6 collective-permute-start.2
  104.3 3.5 collective-permute-start.3
  113.3 8.7 %collective-permute-start.5 = (bf16[2,32,3,34,1]{3,1,4,2,0:T(8,128)(2,1)S(1)}, bf16[2,32,3,34,1]{3,1,4,2,0:T(8,128)(2,1)S(1)}, u32[]{:S(2)}, u32[]{:S(2)}) collective-permute-start(bf16[2,32,3,34,1]{3,1,4,2,0:T(8,128)(2,1)S(1)} %copy.57), channel_id=1, source_target_pairs={{1,0},{2,1},{3,2},{0,3},{5,4},{6,5},{7,6},{4,7},{9,8},{10,9},{11,1... | collective-permute-start | bytes 39176 | tf_op jit(solution)/shard_map/ppermute | solution.py:18
  114.8 4.2 %collective-permute-start.4 = (bf16[2,32,3,34,1]{3,1,4,2,0:T(8,128)(2,1)S(1)}, bf16[2,32,3,34,1]{3,1,4,2,0:T(8,128)(2,1)S(1)}, u32[]{:S(2)}, u32[]{:S(2)}) collective-permute-start(bf16[2,32,3,34,1]{3,1,4,2,0:T(8,128)(2,1)S(1)} %copy.56), channel_id=1, source_target_pairs={{0,1},{1,2},{2,3},{3,0},{4,5},{5,6},{6,7},{7,4},{8,9},{9,10},{10,1... | collective-permute-start | bytes 39176 | tf_op jit(solution)/shard_map/ppermute | solution.py:16
  156.0 2.7 copy-start.29
  156.0 2.7 copy-start.30
  156.0 2.7 copy-start.31
  157.5 2.3 copy-start.26
  162.2 2.4 copy-start.12
  162.2 2.4 copy-start.13
  163.3 2.3 copy-start.6
  163.3 2.3 copy-start.7
  163.3 2.3 copy-start.8
  163.3 2.3 copy-start.9
  163.3 2.3 copy-start.10
  163.3 2.3 copy-start.32
  (16 other events, 31.6 us)
Sparse Core Ops, SparseCore 0:
  156.1 244.2 all-reduce.1
where the time goes:
time: 410 us; the launch traced here: 409 us
  waiting for transfers between devices  238 us (58%)
  blocking collectives  82.2 us (20%)
  matrix products  27.2 us (7%)
  local copies, waits for them, and re-layouts  23.4 us (6%)
  between operations  15.4 us (4%)
  starting transfers between devices  12.2 us (3%)
  other arithmetic  10.7 us (3%)
    psum x1, waiting for transfers between devices, body(): lax.psum((jnp.stack(pieces, 2).reshape(channels, channels, 3, 3, 3), bias...  231 us
    psum x1, blocking collectives, body(): lax.psum((jnp.stack(pieces, 2).reshape(channels, channels, 3, 3, 3), bias...  82.2 us
    dot_general x9, matrix products, body(): jnp.einsum('ock,ckxyz->oxyz', kernel[:, :, step_x, step_y, :], slabs, pre...  13.6 us
    ppermute x3, starting transfers between devices, extended(): lax.ppermute(head, axis, [((i + 1) % count, i) for i in range(count)])  10.6 us
    dot_general x9, matrix products, body(): jnp.einsum('ock,okxyz->cxyz', kernel[:, :, step_x, step_y, :], grad_slabs...  10.3 us
  transfers between devices with their start and end apart: 7, of which 4 were waited for; matrix products, arithmetic and copies ran while one was open for 4% of the time, Pallas kernels for 0%

commit v1 on v0

v1 whole, which is shorter than its diff:
```python
import functools
import math

import jax
import jax.numpy as jnp
from jax import lax
from jax.experimental import pallas as pl
from jax.experimental.pallas import tpu as pltpu
from jax.sharding import PartitionSpec as P

F32 = jnp.float32
BF16 = jnp.bfloat16
MESH = pl.DeviceIdType.MESH
C = 32
ROWS = 32
LANES = 128
TAPS = 9
PLANES = 16
ZS = 8
GROUP = 32
BLOCKS = 36
HALO = 34
TOP, BOTTOM = 0, 33
LEFT, RIGHT = 0, 64


def block(b):
    return pl.ds(b * LANES, LANES)


def kernel(
    scale,
    snap, cot, idx, means, scales, bias, weights,
    o_pred, o_sg, o_kg, o_bias,
    raw_own, raw_n, raw_c, w_raw, flat, xn, xc, d, wp, ws,
    edge, side, edge_in, side_in, pack, pack_in,
    res, out32, out16, kg_acc, kg_own, rs_in, z_own, z_in, ag,
    s_load, s_bulk, r_bulk, s_halo, r_halo, s_pack, r_pack, s_sum, r_sum, s_out,
):
    gx, gy, gz = lax.axis_index("gx"), lax.axis_index("gy"), lax.axis_index("gz")
    ring, high = lax.rem(gx, ZS), gx // ZS
    me = high * 16 + gy * 4 + gz

    def member(k):
        return {"gx": (k // 16) * ZS + ring, "gy": lax.rem(k // 4, 4), "gz": lax.rem(k, 4)}

    def along(k):
        return {"gx": high * ZS + k}

    loads = [
        pltpu.make_async_copy(snap, raw_own.at[0], s_load.at[0]),
        pltpu.make_async_copy(cot, raw_own.at[1], s_load.at[1]),
        pltpu.make_async_copy(weights, w_raw, s_load.at[2]),
    ]
    for copy in loads:
        copy.start()

    next_x = [lax.rem(gx + 1, PLANES), lax.rem(gx + PLANES - 1, PLANES)]
    barrier = pltpu.get_barrier_semaphore()
    for x in next_x:
        pl.semaphore_signal(barrier, inc=1, device_id={"gx": x}, device_id_type=MESH)
    for k in range(1, ZS):
        pl.semaphore_signal(barrier, inc=1, device_id=along(lax.rem(ring + k, ZS)), device_id_type=MESH)
    for k in range(1, GROUP):
        pl.semaphore_signal(barrier, inc=1, device_id=member(lax.rem(me + k, GROUP)), device_id_type=MESH)
    pl.semaphore_wait(barrier, 2 + ZS - 1 + GROUP - 1)

    def bulk(field, source, landing):
        copies = []
        for way in range(2):
            copies.append(
                pltpu.make_async_remote_copy(
                    source, landing.at[way], s_bulk.at[field, way], r_bulk.at[field, way],
                    device_id={"gx": next_x[way]}, device_id_type=MESH,
                )
            )
        return copies

    bulk_n = bulk(0, snap, raw_n)
    for copy in bulk_n:
        copy.start()

    chosen = lax.broadcasted_iota(jnp.int32, means.shape, 1) == idx[...]
    centre = jnp.sum(jnp.where(chosen, means[...], 0.0), 1, keepdims=True)
    spread = 1.0 / jnp.sum(jnp.where(chosen, scales[...], 0.0), 1, keepdims=True)
    centre_b = jnp.broadcast_to(centre, (C, LANES))
    spread_b = jnp.broadcast_to(spread, (C, LANES))
    lane = lax.broadcasted_iota(jnp.int32, (C, LANES), 1)

    def relayout(raw, into, row0, normalise, edges):
        for c in range(0, C, 8):
            flat[pl.ds(c * ROWS, 8 * ROWS), :] = raw[pl.ds(c, 8)].astype(F32).reshape(8 * ROWS, LANES)

        def step(y, carry):
            v = flat[pl.ds(y, C, stride=ROWS), :]
            if normalise:
                v = (v - centre_b) * spread_b
            into[pl.ds(row0, C), pl.ds(pl.multiple_of((y + 1) * LANES, LANES), LANES)] = v.astype(BF16)
            if edges:
                last, first = carry
                last = jnp.where(lane == LEFT + 1 + y, pltpu.roll(v, lax.rem(y + LEFT + 2, LANES), 1), last)
                first = jnp.where(lane == RIGHT + 1 + y, pltpu.roll(v, y + RIGHT + 1, 1), first)
                carry = (last, first)
            return carry

        zero = jnp.zeros((C, LANES), F32)
        return lax.fori_loop(0, ROWS, step, (zero, zero) if edges else 0, unroll=4)

    fields = (xn, xc)
    for f in range(2):
        loads[f].wait()
        last, first = relayout(raw_own.at[f], fields[f], C, f == 0, True)
        side[0, f] = last.astype(BF16)
        side[1, f] = first.astype(BF16)
        edge[0, f] = fields[f][pl.ds(C, C), block(1)]
        edge[1, f] = fields[f][pl.ds(C, C), block(ROWS)]

    halo = []
    for e in range(2):
        y = lax.rem(gy + (3 if e == 0 else 1), 4)
        for k in range(3):
            z = lax.rem(gz + k + 3, 4)
            halo.append(
                pltpu.make_async_remote_copy(
                    edge.at[e], edge_in.at[e, 2 - k], s_halo.at[e, k], r_halo.at[e, 2 - k],
                    device_id={"gy": y, "gz": z}, device_id_type=MESH,
                )
            )
    for k in range(2):
        z = lax.rem(gz + (1 if k == 0 else 3), 4)
        halo.append(
            pltpu.make_async_remote_copy(
                side.at[k], side_in.at[k], s_halo.at[2, k], r_halo.at[2, k],
                device_id={"gz": z}, device_id_type=MESH,
            )
        )
    for copy in halo:
        copy.start()

    loads[2].wait()
    rows_i = lax.broadcasted_iota(jnp.int32, (C, 3 * C), 0)
    cols_i = lax.broadcasted_iota(jnp.int32, (C, 3 * C), 1)
    places = [(cols_i == rows_i + a * C).astype(BF16) for a in range(3)]
    eye = (lax.broadcasted_iota(jnp.int32, (C, C), 0) == lax.broadcasted_iota(jnp.int32, (C, C), 1)).astype(BF16)
    for be in range(TAPS):
        total = jnp.zeros((C, 3 * C), F32)
        for a in range(3):
            total = total + jnp.dot(w_raw[a * TAPS + be], places[a], preferred_element_type=F32)
        wp[pl.ds(be * C, C), :] = total.astype(BF16)
        stack = jnp.concatenate([w_raw[(2 - a) * TAPS + TAPS - 1 - be] for a in range(3)], 0)
        turned = lax.dot_general(eye, stack, (((1,), (1,)), ((), ())), preferred_element_type=F32)
        ws[pl.ds(be * C, C), :] = turned.astype(BF16)
    xn[pl.ds(3 * C, C), :] = jnp.ones((C, BLOCKS * LANES), BF16)

    for copy in halo:
        copy.wait()
    above = (gy > 0).astype(F32)
    below = (gy < 3).astype(F32)
    halo_c = None
    for f in range(2):
        row_top = edge_in[1, 1, f].astype(F32) * above
        row_bottom = edge_in[0, 1, f].astype(F32) * below
        h = side_in[0, f].astype(F32) + side_in[1, f].astype(F32)
        h = jnp.where(lane == LEFT, pltpu.roll(edge_in[1, 0, f].astype(F32) * above, LEFT + 1, 1), h)
        h = jnp.where(lane == LEFT + 33, pltpu.roll(edge_in[0, 0, f].astype(F32) * below, LEFT + 34, 1), h)
        h = jnp.where(lane == RIGHT, pltpu.roll(edge_in[1, 2, f].astype(F32) * above, RIGHT, 1), h)
        h = jnp.where(lane == RIGHT + 33, pltpu.roll(edge_in[0, 2, f].astype(F32) * below, RIGHT + 33, 1), h)
        for i, (b, v) in enumerate(((TOP, row_top), (BOTTOM, row_bottom), (HALO, h))):
            v16 = v.astype(BF16)
            fields[f][pl.ds(C, C), block(b)] = v16
            pack[f, i] = v16
        if f == 1:
            halo_c = h
    packs = []
    for way in range(2):
        packs.append(
            pltpu.make_async_remote_copy(
                pack, pack_in.at[way], s_pack.at[way], r_pack.at[way],
                device_id={"gx": next_x[way]}, device_id_type=MESH,
            )
        )
    for copy in packs:
        copy.start()

    def shifted(r, carry):
        at = pl.ds(pl.multiple_of(r * LANES, LANES), LANES)
        v16 = xc[pl.ds(C, C), at]
        v = v16.astype(F32)
        up = jnp.where(lane == LANES - 1, pltpu.roll(halo_c, LANES - 1 - RIGHT - r, 1), pltpu.roll(v, LANES - 1, 1))
        down = jnp.where(lane == 0, pltpu.roll(halo_c, lax.rem(LANES - LEFT - r, LANES), 1), pltpu.roll(v, 1, 1))
        d[pl.ds(0, C), at] = up.astype(BF16)
        d[pl.ds(C, C), at] = v16
        d[pl.ds(2 * C, C), at] = down.astype(BF16)
        return carry

    lax.fori_loop(0, 34, shifted, 0, unroll=2)

    for way, copy in enumerate(bulk_n):
        copy.wait()
    bulk_c = bulk(1, cot, raw_c)
    for copy in bulk_c:
        copy.start()
    for way in range(2):
        relayout(raw_n.at[way], xn, way * 2 * C, True, False)

    span = 8 * LANES
    kg_acc[...] = jnp.zeros_like(kg_acc)

    def gather(k, carry):
        start = k * span
        left = jnp.concatenate(
            [d[:, pl.ds(pl.multiple_of(start + (2 - b) * LANES, LANES), span)] for b in range(3)], 0
        )
        right = xn[:, pl.ds(pl.multiple_of(start + LANES, LANES), span)]
        kg_acc[...] += lax.dot_general(left, right, (((1,), (1,)), ((), ())), preferred_element_type=F32)
        return carry

    lax.fori_loop(0, ROWS * LANES // span, gather, 0)
    for be in range(TAPS):
        kg_own[:, be, :] = kg_acc[pl.ds(be * C, C), :]

    def spread_out(source, landing, slot, stage, count, mine, device):
        for k in range(1, count):
            peer = lax.rem(mine + count // 2 + k - 1 + (1 if k > count // 2 else 0), count)
            peer = lax.rem(mine + k, count)
            pltpu.make_async_remote_copy(
                source(peer), landing.at[slot], s_sum.at[stage], r_sum.at[stage],
                device_id=device(peer), device_id_type=MESH,
            ).start()

    def arrived(landing, stage, count):
        all_of = landing.at[pl.ds(0, count - 1)]
        pltpu.make_async_copy(all_of, all_of, r_sum.at[stage]).wait()
        pltpu.make_async_copy(all_of, all_of, s_sum.at[stage]).wait()

    spread_out(lambda p: kg_own.at[p], rs_in, me, 0, GROUP, me, member)
    rs_in[me] = kg_own[me]

    def convolve(x, filters, finish, target, field):
        def chunk(k, carry):
            at = pl.ds(pl.multiple_of(k * 4 * LANES, 4 * LANES), 4 * LANES)
            res[:, at] = jnp.dot(filters[...], x[pl.ds(0, 3 * C), at], preferred_element_type=F32)
            return carry

        lax.fori_loop(0, BLOCKS // 4, chunk, 0)

        def of(b, e):
            return pl.ds((b * 3 + e) * C, C)

        left = res[of(0, 0), block(HALO)]
        right = res[of(0, 2), block(HALO)]
        for b in range(1, 3):
            left = left + pltpu.roll(res[of(b, 0), block(HALO)], LANES - b, 1)
            right = right + pltpu.roll(res[of(b, 2), block(HALO)], LANES - b, 1)

        def row(y, carry):
            s = []
            for e in range(3):
                total = None
                for b in range(3):
                    part = res[of(b, e), pl.ds(pl.multiple_of((y + b) * LANES, LANES), LANES)]
                    total = part if total is None else total + part
                s.append(total)
            from_left = jnp.where(lane == 0, pltpu.roll(left, lax.rem(LANES - y, LANES), 1), pltpu.roll(s[0], 1, 1))
            from_right = jnp.where(
                lane == LANES - 1, pltpu.roll(right, LANES - 1 - RIGHT - y, 1), pltpu.roll(s[2], LANES - 1, 1)
            )
            out32[pl.ds(y, C, stride=ROWS), :] = finish(s[1] + from_left + from_right)
            return carry

        lax.fori_loop(0, ROWS, row, 0, unroll=2)
        for c in range(0, C, 8):
            out16[field, pl.ds(c, 8)] = out32[pl.ds(c * ROWS, 8 * ROWS), :].reshape(8, ROWS, LANES).astype(BF16)
        copy = pltpu.make_async_copy(out16.at[field], target, s_out.at[field])
        copy.start()
        return copy

    for copy in packs:
        copy.wait()
    for way in range(2):
        for f in range(2):
            for i, b in enumerate((TOP, BOTTOM, HALO)):
                fields[f][pl.ds(way * 2 * C, C), block(b)] = pack_in[way, f, i]
    zero16 = jnp.zeros((3 * C, LANES), BF16)
    for x in fields:
        x[pl.ds(0, 3 * C), block(BLOCKS - 1)] = zero16

    eye32 = lax.broadcasted_iota(jnp.int32, (C, C), 0) == lax.broadcasted_iota(jnp.int32, (C, C), 1)
    bias_col = jnp.sum(jnp.where(eye32, jnp.broadcast_to(bias[...], (C, C)), 0.0), 1, keepdims=True)
    bias_b = jnp.broadcast_to(bias_col, (C, LANES))
    written = [convolve(xn, wp, lambda v: v + bias_b, o_pred, 0)]

    arrived(rs_in, 0, GROUP)
    total = rs_in[0]
    for k in range(1, GROUP):
        total = total + rs_in[k]
    z_own[...] = total
    spread_out(lambda p: z_own, z_in, ring, 1, ZS, ring, along)
    z_in[ring] = total

    for copy in bulk_c:
        copy.wait()
    for way in range(2):
        relayout(raw_c.at[way], xc, way * 2 * C, False, False)
    written.append(convolve(xc, ws, lambda v: v * spread_b, o_sg, 1))

    arrived(z_in, 1, ZS)
    total = z_in[0]
    for k in range(1, ZS):
        total = total + z_in[k]
    ag[me] = total * scale
    spread_out(lambda p: ag.at[me], ag, me, 2, GROUP, me, member)
    arrived(ag, 2, GROUP)
    for be in range(TAPS):
        v = ag[:, be, :]
        for a in range(3):
            turned = v if a == 0 else pltpu.roll(v, LANES - a * C, 1)
            o_kg[a * TAPS + be] = turned[:, :C]
        if be == 4:
            column = jnp.broadcast_to(v[:, 3 * C : 3 * C + 1], (C, C))
            o_bias[...] = jnp.sum(jnp.where(eye32, column, 0.0), 0, keepdims=True)
    for copy in written:
        copy.wait()


def body(snapshot, snap_index, snap_means, snap_scales, out_bias, weights, cotangent):
    cells = PLANES * 4 * ROWS * 4 * LANES
    scale = 1.0 / math.sqrt(cells)
    shape = jax.ShapeDtypeStruct
    dma = pltpu.SemaphoreType.DMA
    vmem = pltpu.VMEM
    hbm = pl.BlockSpec(memory_space=pl.ANY)
    local = pl.BlockSpec(memory_space=pltpu.VMEM)
    tile = (C, LANES)
    pred, sg, kg, bias = pl.pallas_call(
        functools.partial(kernel, scale),
        out_shape=(
            shape((C, ROWS, LANES), BF16),
            shape((C, ROWS, LANES), BF16),
            shape((27, C, C), F32),
            shape((1, C), F32),
        ),
        in_specs=[hbm, hbm, local, local, local, local, hbm],
        out_specs=(hbm, hbm, local, local),
        scratch_shapes=[
            vmem((2, C, ROWS, LANES), BF16),
            vmem((2, C, ROWS, LANES), BF16),
            vmem((2, C, ROWS, LANES), BF16),
            vmem((27, C, C), BF16),
            vmem((C * ROWS, LANES), F32),
            vmem((4 * C, BLOCKS * LANES), BF16),
            vmem((3 * C, BLOCKS * LANES), BF16),
            vmem((3 * C, BLOCKS * LANES), BF16),
            vmem((TAPS * C, 3 * C), BF16),
            vmem((TAPS * C, 3 * C), BF16),
            vmem((2, 2) + tile, BF16),
            vmem((2, 2) + tile, BF16),
            vmem((2, 3, 2) + tile, BF16),
            vmem((2, 2) + tile, BF16),
            vmem((2, 3) + tile, BF16),
            vmem((2, 2, 3) + tile, BF16),
            vmem((TAPS * C, BLOCKS * LANES), F32),
            vmem((C * ROWS, LANES), F32),
            vmem((2, C, ROWS, LANES), BF16),
            vmem((TAPS * C, LANES), F32),
            vmem((GROUP, TAPS, LANES), F32),
            vmem((GROUP, TAPS, LANES), F32),
            vmem((TAPS, LANES), F32),
            vmem((ZS, TAPS, LANES), F32),
            vmem((GROUP, TAPS, LANES), F32),
            dma((3,)),
            dma((2, 2)),
            dma((2, 2)),
            dma((3, 3)),
            dma((3, 3)),
            dma((2,)),
            dma((2,)),
            dma((3,)),
            dma((3,)),
            dma((2,)),
        ],
        compiler_params=pltpu.CompilerParams(
            collective_id=0, has_side_effects=True, vmem_limit_bytes=32 * 2**20
        ),
    )(
        snapshot.reshape(C, ROWS, LANES),
        cotangent.reshape(C, ROWS, LANES),
        snap_index.reshape(1, 1),
        snap_means.T,
        snap_scales.T,
        out_bias.reshape(1, C),
        weights.transpose(2, 3, 4, 0, 1).reshape(27, C, C),
    )
    return (
        pred.reshape(C, 1, ROWS, LANES),
        sg.reshape(C, 1, ROWS, LANES),
        kg.reshape(3, 3, 3, C, C).transpose(3, 4, 0, 1, 2),
        bias.reshape(C),
    )


def solution(mesh):
    split = P(None, "gx", "gy", "gz")
    in_specs = (split, P(), P(), P(), P(), P(), split)
    out_specs = (split, split, P(), P())
    return jax.shard_map(body, mesh=mesh, in_specs=in_specs, out_specs=out_specs, check_vma=False)
```

time: 410 us -> 52.7 us (0.13)
  waiting for transfers between devices: 238 us -> 0 us
  blocking collectives: 82.2 us -> 0 us
  Pallas kernels: 0 us -> 43.5 us
  matrix products: 27.2 us -> 0 us
  local copies, waits for them, and re-layouts: 23.4 us -> 7.6 us
  between operations: 15.4 us -> 1.3 us
  starting transfers between devices: 12.2 us -> 0 us
  other arithmetic: 10.7 us -> 0 us
    psum x1 -> x0, waiting for transfers between devices: 231 us -> none  [body(): lax.psum((jnp.stack(pieces, 2).reshape(channels, channels, 3, 3, 3), bias...]
    psum x1 -> x0, blocking collectives: 82.2 us -> none  [body(): lax.psum((jnp.stack(pieces, 2).reshape(channels, channels, 3, 3, 3), bias...]
    pallas_call x0 -> x1, Pallas kernels: none -> 43.5 us  [body(): pl.pallas_call(functools.partial(kernel, scale), out_shape=(shape((C, ROW...]
    dot_general x27 -> x0, matrix products: 27.2 us -> none  [the longest x9 13.6 us: body(): jnp.einsum('ock,ckxyz->oxyz', kernel[:, :, step_x, step_y, :], slabs, pre...]
    ppermute x6 -> x0, starting transfers between devices: 12.1 us -> none  [the longest x3 10.6 us: extended(): lax.ppermute(head, axis, [((i + 1) % count, i) for i in range(count)])]
    ppermute x6 -> x0, waiting for transfers between devices: 7.12 us -> none  [the longest x3 4.77 us: extended(): lax.ppermute(tail, axis, [(i, (i + 1) % count) for i in range(count)])]
    another operation x4 -> x0, local copies, waits for them, and re-layouts: 6.33 us -> none  [window(): return jnp.stack(slabs, 1)]
    ppermute x2 -> x0, local copies, waits for them, and re-layouts: 6.01 us -> none  [the longest x1 3.02 us: extended(): lax.ppermute(head, axis, [((i + 1) % count, i) for i in range(count)])]
  transfers between devices with their start and end apart: 7 -> 0, of which waited for: 4 -> 0; matrix products, arithmetic and copies ran while one was open for 4% -> 0% of each run, Pallas kernels for 0% -> 0%
where the time goes in v1:
time: 52.7 us; the launch traced here: 52.4 us
  Pallas kernels  43.5 us (83%)
  local copies, waits for them, and re-layouts  7.6 us (14%)
  between operations  1.3 us (2%)
    pallas_call x1, Pallas kernels, body(): pl.pallas_call(functools.partial(kernel, scale), out_shape=(shape((C, ROW...  43.5 us
    unnamed x16, local copies, waits for them, and re-layouts  7.6 us

profile of v1, /device:TPU:1, one launch (start us, length us, event | category | flops | bytes accessed | tf_op | source)
XLA Modules:
  0.0 52.4 jit_solution(10841351509743917979)
XLA Ops:
  1.3 0.0 copy-start.5
  1.3 0.6 %copy-done.5 = f32[32]{0:T(128)S(1)} copy-done((f32[32]{0:T(128)S(1)}, f32[32]{0:T(128)}, u32[]{:S(2)}) %copy-start.5) | copy-done | bytes 152
  1.9 0.0 copy-start
  1.9 0.9 %copy-done = bf16[32,1,32,128]{3,2,1,0:T(8,128)(2,1)S(1)} copy-done((bf16[32,1,32,128]{3,2,1,0:T(8,128)(2,1)S(1)}, bf16[32,1,32,128]{3,2,1,0:T(8,128)(2,1)}, u32[]{:S(2)}) %copy-start) | copy-done | bytes 262168
  2.9 0.0 copy-start.1
  2.9 0.9 %copy-done.1 = bf16[32,1,32,128]{3,2,1,0:T(8,128)(2,1)S(1)} copy-done((bf16[32,1,32,128]{3,2,1,0:T(8,128)(2,1)S(1)}, bf16[32,1,32,128]{3,2,1,0:T(8,128)(2,1)}, u32[]{:S(2)}) %copy-start.1) | copy-done | bytes 262168
  3.8 0.0 copy-start.2
  3.8 0.9 %copy-done.2 = bf16[32,32,3,3,3]{1,0,4,3,2:T(8,128)(2,1)S(1)} copy-done((bf16[32,32,3,3,3]{1,0,4,3,2:T(8,128)(2,1)S(1)}, bf16[32,32,3,3,3]{1,0,4,3,2:T(8,128)(2,1)}, u32[]{:S(2)}) %copy-start.2) | copy-done | bytes 55320
  4.8 0.0 copy-start.3
  4.8 0.7 %copy-done.3 = f32[64,32]{0,1:T(8,128)S(1)} copy-done((f32[64,32]{0,1:T(8,128)S(1)}, f32[64,32]{0,1:T(8,128)}, u32[]{:S(2)}) %copy-start.3) | copy-done | bytes 8216
  5.5 0.0 copy-start.4
  5.5 0.7 %copy-done.4 = f32[64,32]{0,1:T(8,128)S(1)} copy-done((f32[64,32]{0,1:T(8,128)S(1)}, f32[64,32]{0,1:T(8,128)}, u32[]{:S(2)}) %copy-start.4) | copy-done | bytes 8216
  6.2 43.5 %shard_map.102 = (bf16[32,32,128]{2,1,0:T(8,128)(2,1)S(1)}, bf16[32,32,128]{2,1,0:T(8,128)(2,1)S(1)}, f32[27,32,32]{2,1,0:T(8,128)S(1)}, f32[1,32]{1,0:T(1,128)S(1)}) custom-call(bf16[32,32,128]{2,1,0:T(8,128)(2,1)S(1)} %bitcast.21, bf16[32,32,128]{2,1,0:T(8,128)(2,1)S(1)} %bitcast.22, s32[1,1]{1,0:T(1,128)} %bitcast.19.idx, f32[32,64]{1,0:T(8,128)S(1)} %bitcast.26, ...), custom_call_target="tpu_custom_call" | custom-call | tf_op jit(solution)/shard_map/pallas_call | solution.py:335
  49.7 0.7 %copy.18 = bf16[32,1,32,128]{3,2,1,0:T(8,128)(2,1)} copy(bf16[32,1,32,128]{3,2,1,0:T(8,128)(2,1)S(1)} %bitcast.24) | data formatting | bytes 524288
  50.4 0.7 %copy.19 = bf16[32,1,32,128]{3,2,1,0:T(8,128)(2,1)} copy(bf16[32,1,32,128]{3,2,1,0:T(8,128)(2,1)S(1)} %bitcast.23) | data formatting | bytes 524288
  51.1 0.8 %copy.20 = f32[32,32,3,3,3]{1,0,4,3,2:T(8,128)} copy(f32[32,32,3,3,3]{1,0,4,3,2:T(8,128)S(1)} %bitcast.20) | data formatting | bytes 221184
  51.9 0.5 copy.21
Async XLA Ops:
  1.3 0.7 %copy-start.5 = (f32[32]{0:T(128)S(1)}, f32[32]{0:T(128)}, u32[]{:S(2)}) copy-start(f32[32]{0:T(128)} %param.11) | copy-start | bytes 388
  1.9 0.9 %copy-start = (bf16[32,1,32,128]{3,2,1,0:T(8,128)(2,1)S(1)}, bf16[32,1,32,128]{3,2,1,0:T(8,128)(2,1)}, u32[]{:S(2)}) copy-start(bf16[32,1,32,128]{3,2,1,0:T(8,128)(2,1)} %param.7) | copy-start | bytes 786436
  2.9 0.9 %copy-start.1 = (bf16[32,1,32,128]{3,2,1,0:T(8,128)(2,1)S(1)}, bf16[32,1,32,128]{3,2,1,0:T(8,128)(2,1)}, u32[]{:S(2)}) copy-start(bf16[32,1,32,128]{3,2,1,0:T(8,128)(2,1)} %param.13) | copy-start | bytes 786436
  3.8 0.9 %copy-start.2 = (bf16[32,32,3,3,3]{1,0,4,3,2:T(8,128)(2,1)S(1)}, bf16[32,32,3,3,3]{1,0,4,3,2:T(8,128)(2,1)}, u32[]{:S(2)}) copy-start(bf16[32,32,3,3,3]{1,0,4,3,2:T(8,128)(2,1)} %param.12) | copy-start | bytes 165892
  4.8 0.7 %copy-start.3 = (f32[64,32]{0,1:T(8,128)S(1)}, f32[64,32]{0,1:T(8,128)}, u32[]{:S(2)}) copy-start(f32[64,32]{0,1:T(8,128)} %param.9) | copy-start | bytes 24580
  5.5 0.7 %copy-start.4 = (f32[64,32]{0,1:T(8,128)S(1)}, f32[64,32]{0,1:T(8,128)}, u32[]{:S(2)}) copy-start(f32[64,32]{0,1:T(8,128)} %param.10) | copy-start | bytes 24580

commit v2 on v1

--- a/solution.py
+++ b/solution.py
@@ -18,7 +18,8 @@
 PLANES = 16
 ZS = 8
 GROUP = 32
-BLOCKS = 36
+BLOCKS = 35
+HALF = ROWS // 2
 HALO = 34
 TOP, BOTTOM = 0, 33
 LEFT, RIGHT = 0, 64
@@ -30,9 +31,9 @@
 
 def kernel(
     scale,
-    snap, cot, idx, means, scales, bias, weights,
+    snap, cot, idx_in, means_in, scales_in, bias_in, weights,
     o_pred, o_sg, o_kg, o_bias,
-    raw_own, raw_n, raw_c, w_raw, flat, xn, xc, d, wp, ws,
+    raw_own, raw_n, raw_c, w_raw, idx, means, scales, bias, flat, xn, xc, d, wp, ws,
     edge, side, edge_in, side_in, pack, pack_in,
     res, out32, out16, kg_acc, kg_own, rs_in, z_own, z_in, ag,
     s_load, s_bulk, r_bulk, s_halo, r_halo, s_pack, r_pack, s_sum, r_sum, s_out,
@@ -51,6 +52,10 @@
         pltpu.make_async_copy(snap, raw_own.at[0], s_load.at[0]),
         pltpu.make_async_copy(cot, raw_own.at[1], s_load.at[1]),
         pltpu.make_async_copy(weights, w_raw, s_load.at[2]),
+        pltpu.make_async_copy(idx_in, idx, s_load.at[3]),
+        pltpu.make_async_copy(means_in, means, s_load.at[4]),
+        pltpu.make_async_copy(scales_in, scales, s_load.at[5]),
+        pltpu.make_async_copy(bias_in, bias, s_load.at[6]),
     ]
     for copy in loads:
         copy.start()
@@ -67,19 +72,24 @@
 
     def bulk(field, source, landing):
         copies = []
-        for way in range(2):
-            copies.append(
-                pltpu.make_async_remote_copy(
-                    source, landing.at[way], s_bulk.at[field, way], r_bulk.at[field, way],
-                    device_id={"gx": next_x[way]}, device_id_type=MESH,
+        for half in range(2):
+            for way in range(2):
+                copies.append(
+                    pltpu.make_async_remote_copy(
+                        source.at[:, pl.ds(half * HALF, HALF)], landing.at[way, half],
+                        s_bulk.at[field, way, half], r_bulk.at[field, way, half],
+                        device_id={"gx": next_x[way]}, device_id_type=MESH,
+                    )
                 )
-            )
         return copies
 
     bulk_n = bulk(0, snap, raw_n)
+    bulk_c = bulk(1, cot, raw_c)
     for copy in bulk_n:
         copy.start()
 
+    for copy in loads[3:]:
+        copy.wait()
     chosen = lax.broadcasted_iota(jnp.int32, means.shape, 1) == idx[...]
     centre = jnp.sum(jnp.where(chosen, means[...], 0.0), 1, keepdims=True)
     spread = 1.0 / jnp.sum(jnp.where(chosen, scales[...], 0.0), 1, keepdims=True)
@@ -87,29 +97,25 @@
     spread_b = jnp.broadcast_to(spread, (C, LANES))
     lane = lax.broadcasted_iota(jnp.int32, (C, LANES), 1)
 
-    def relayout(raw, into, row0, normalise, edges):
+    def relayout(raw, flat, into, row0, start, rows, normalise, edges):
         for c in range(0, C, 8):
-            flat[pl.ds(c * ROWS, 8 * ROWS), :] = raw[pl.ds(c, 8)].astype(F32).reshape(8 * ROWS, LANES)
-
-        def step(y, carry):
-            v = flat[pl.ds(y, C, stride=ROWS), :]
+            flat[pl.ds(c * rows, 8 * rows), :] = raw[pl.ds(c, 8)].astype(F32).reshape(8 * rows, LANES)
+        last = first = jnp.zeros((C, LANES), F32)
+        for k in range(rows):
+            y = start + k
+            v = flat[pl.ds(k, C, stride=rows), :]
             if normalise:
                 v = (v - centre_b) * spread_b
-            into[pl.ds(row0, C), pl.ds(pl.multiple_of((y + 1) * LANES, LANES), LANES)] = v.astype(BF16)
+            into[pl.ds(row0, C), block(y + 1)] = v.astype(BF16)
             if edges:
-                last, first = carry
-                last = jnp.where(lane == LEFT + 1 + y, pltpu.roll(v, lax.rem(y + LEFT + 2, LANES), 1), last)
+                last = jnp.where(lane == LEFT + 1 + y, pltpu.roll(v, y + LEFT + 2, 1), last)
                 first = jnp.where(lane == RIGHT + 1 + y, pltpu.roll(v, y + RIGHT + 1, 1), first)
-                carry = (last, first)
-            return carry
-
-        zero = jnp.zeros((C, LANES), F32)
-        return lax.fori_loop(0, ROWS, step, (zero, zero) if edges else 0, unroll=4)
+        return last, first
 
     fields = (xn, xc)
     for f in range(2):
         loads[f].wait()
-        last, first = relayout(raw_own.at[f], fields[f], C, f == 0, True)
+        last, first = relayout(raw_own.at[f], flat.at[f], fields[f], C, 0, ROWS, f == 0, True)
         side[0, f] = last.astype(BF16)
         side[1, f] = first.astype(BF16)
         edge[0, f] = fields[f][pl.ds(C, C), block(1)]
@@ -182,47 +188,47 @@
     for copy in packs:
         copy.start()
 
-    def shifted(r, carry):
-        at = pl.ds(pl.multiple_of(r * LANES, LANES), LANES)
-        v16 = xc[pl.ds(C, C), at]
+    for r in range(ROWS + 2):
+        v16 = xc[pl.ds(C, C), block(r)]
         v = v16.astype(F32)
         up = jnp.where(lane == LANES - 1, pltpu.roll(halo_c, LANES - 1 - RIGHT - r, 1), pltpu.roll(v, LANES - 1, 1))
-        down = jnp.where(lane == 0, pltpu.roll(halo_c, lax.rem(LANES - LEFT - r, LANES), 1), pltpu.roll(v, 1, 1))
-        d[pl.ds(0, C), at] = up.astype(BF16)
-        d[pl.ds(C, C), at] = v16
-        d[pl.ds(2 * C, C), at] = down.astype(BF16)
-        return carry
-
-    lax.fori_loop(0, 34, shifted, 0, unroll=2)
-
-    for way, copy in enumerate(bulk_n):
-        copy.wait()
-    bulk_c = bulk(1, cot, raw_c)
-    for copy in bulk_c:
-        copy.start()
-    for way in range(2):
-        relayout(raw_n.at[way], xn, way * 2 * C, True, False)
-
-    span = 8 * LANES
-    kg_acc[...] = jnp.zeros_like(kg_acc)
-
-    def gather(k, carry):
-        start = k * span
-        left = jnp.concatenate(
-            [d[:, pl.ds(pl.multiple_of(start + (2 - b) * LANES, LANES), span)] for b in range(3)], 0
-        )
-        right = xn[:, pl.ds(pl.multiple_of(start + LANES, LANES), span)]
-        kg_acc[...] += lax.dot_general(left, right, (((1,), (1,)), ((), ())), preferred_element_type=F32)
-        return carry
-
-    lax.fori_loop(0, ROWS * LANES // span, gather, 0)
+        down = jnp.where(lane == 0, pltpu.roll(halo_c, (LANES - LEFT - r) % LANES, 1), pltpu.roll(v, 1, 1))
+        d[pl.ds(0, C), block(r)] = up.astype(BF16)
+        d[pl.ds(C, C), block(r)] = v16
+        d[pl.ds(2 * C, C), block(r)] = down.astype(BF16)
+
+    span = HALF * LANES
+    total = None
+    for half in range(2):
+        for way in range(2):
+            bulk_n[2 * half + way].wait()
+        for way in range(2):
+            relayout(
+                raw_n.at[way, half], flat.at[way, pl.ds(half * C * HALF, C * HALF)],
+                xn, way * 2 * C, half * HALF, HALF, True, False,
+            )
+        start = half * span
+        left = jnp.concatenate([d[:, pl.ds(start + (2 - b) * LANES, span)] for b in range(3)], 0)
+        right = xn[:, pl.ds(start + LANES, span)]
+        part = lax.dot_general(left, right, (((1,), (1,)), ((), ())), preferred_element_type=F32)
+        if half == 0:
+            kg_acc[...] = part
+        else:
+            kg_acc[...] += part
     for be in range(TAPS):
         kg_own[:, be, :] = kg_acc[pl.ds(be * C, C), :]
 
-    def spread_out(source, landing, slot, stage, count, mine, device):
-        for k in range(1, count):
-            peer = lax.rem(mine + count // 2 + k - 1 + (1 if k > count // 2 else 0), count)
-            peer = lax.rem(mine + k, count)
+    near = {0: 0, 1: 1, 2: 2, 3: 1}
+    steps = [(dy, dc, dx) for dy in range(4) for dc in range(2) for dx in range(4)][1:]
+    steps.sort(key=lambda t: -(4 * (near[t[0]] + near[t[2]]) + t[1]))
+    y, core = high * 2 + gy // 2, lax.rem(gy, 2)
+    group_peers = [
+        lax.rem(y + dy, 4) * 8 + lax.rem(core + dc, 2) * 4 + lax.rem(gz + dx, 4) for dy, dc, dx in steps
+    ]
+    ring_peers = [lax.rem(ring + k, ZS) for k in (4, 3, 5, 2, 6, 1, 7)]
+
+    def spread_out(source, landing, slot, stage, peers, device):
+        for peer in peers:
             pltpu.make_async_remote_copy(
                 source(peer), landing.at[slot], s_sum.at[stage], r_sum.at[stage],
                 device_id=device(peer), device_id_type=MESH,
@@ -233,16 +239,13 @@
         pltpu.make_async_copy(all_of, all_of, r_sum.at[stage]).wait()
         pltpu.make_async_copy(all_of, all_of, s_sum.at[stage]).wait()
 
-    spread_out(lambda p: kg_own.at[p], rs_in, me, 0, GROUP, me, member)
+    spread_out(lambda p: kg_own.at[p], rs_in, me, 0, group_peers, member)
+    for copy in bulk_c[:2]:
+        copy.start()
     rs_in[me] = kg_own[me]
 
     def convolve(x, filters, finish, target, field):
-        def chunk(k, carry):
-            at = pl.ds(pl.multiple_of(k * 4 * LANES, 4 * LANES), 4 * LANES)
-            res[:, at] = jnp.dot(filters[...], x[pl.ds(0, 3 * C), at], preferred_element_type=F32)
-            return carry
-
-        lax.fori_loop(0, BLOCKS // 4, chunk, 0)
+        res[...] = jnp.dot(filters[...], x[pl.ds(0, 3 * C), :], preferred_element_type=F32)
 
         def of(b, e):
             return pl.ds((b * 3 + e) * C, C)
@@ -253,24 +256,15 @@
             left = left + pltpu.roll(res[of(b, 0), block(HALO)], LANES - b, 1)
             right = right + pltpu.roll(res[of(b, 2), block(HALO)], LANES - b, 1)
 
-        def row(y, carry):
-            s = []
-            for e in range(3):
-                total = None
-                for b in range(3):
-                    part = res[of(b, e), pl.ds(pl.multiple_of((y + b) * LANES, LANES), LANES)]
-                    total = part if total is None else total + part
-                s.append(total)
-            from_left = jnp.where(lane == 0, pltpu.roll(left, lax.rem(LANES - y, LANES), 1), pltpu.roll(s[0], 1, 1))
+        for y in range(ROWS):
+            s = [sum(res[of(b, e), block(y + b)] for b in range(3)) for e in range(3)]
+            from_left = jnp.where(lane == 0, pltpu.roll(left, (LANES - y) % LANES, 1), pltpu.roll(s[0], 1, 1))
             from_right = jnp.where(
                 lane == LANES - 1, pltpu.roll(right, LANES - 1 - RIGHT - y, 1), pltpu.roll(s[2], LANES - 1, 1)
             )
-            out32[pl.ds(y, C, stride=ROWS), :] = finish(s[1] + from_left + from_right)
-            return carry
-
-        lax.fori_loop(0, ROWS, row, 0, unroll=2)
+            out32[field, pl.ds(y, C, stride=ROWS), :] = finish(s[1] + from_left + from_right)
         for c in range(0, C, 8):
-            out16[field, pl.ds(c, 8)] = out32[pl.ds(c * ROWS, 8 * ROWS), :].reshape(8, ROWS, LANES).astype(BF16)
+            out16[field, pl.ds(c, 8)] = out32[field, pl.ds(c * ROWS, 8 * ROWS), :].reshape(8, ROWS, LANES).astype(BF16)
         copy = pltpu.make_async_copy(out16.at[field], target, s_out.at[field])
         copy.start()
         return copy
@@ -281,9 +275,6 @@
         for f in range(2):
             for i, b in enumerate((TOP, BOTTOM, HALO)):
                 fields[f][pl.ds(way * 2 * C, C), block(b)] = pack_in[way, f, i]
-    zero16 = jnp.zeros((3 * C, LANES), BF16)
-    for x in fields:
-        x[pl.ds(0, 3 * C), block(BLOCKS - 1)] = zero16
 
     eye32 = lax.broadcasted_iota(jnp.int32, (C, C), 0) == lax.broadcasted_iota(jnp.int32, (C, C), 1)
     bias_col = jnp.sum(jnp.where(eye32, jnp.broadcast_to(bias[...], (C, C)), 0.0), 1, keepdims=True)
@@ -295,21 +286,27 @@
     for k in range(1, GROUP):
         total = total + rs_in[k]
     z_own[...] = total
-    spread_out(lambda p: z_own, z_in, ring, 1, ZS, ring, along)
+    spread_out(lambda p: z_own, z_in, ring, 1, ring_peers, along)
+    for copy in bulk_c[2:]:
+        copy.start()
     z_in[ring] = total
-
-    for copy in bulk_c:
-        copy.wait()
-    for way in range(2):
-        relayout(raw_c.at[way], xc, way * 2 * C, False, False)
-    written.append(convolve(xc, ws, lambda v: v * spread_b, o_sg, 1))
 
     arrived(z_in, 1, ZS)
     total = z_in[0]
     for k in range(1, ZS):
         total = total + z_in[k]
     ag[me] = total * scale
-    spread_out(lambda p: ag.at[me], ag, me, 2, GROUP, me, member)
+    spread_out(lambda p: ag.at[me], ag, me, 2, group_peers, member)
+    for copy in bulk_c:
+        copy.wait()
+    for way in range(2):
+        for half in range(2):
+            relayout(
+                raw_c.at[way, half], flat.at[way, pl.ds(half * C * HALF, C * HALF)],
+                xc, way * 2 * C, half * HALF, HALF, False, False,
+            )
+    written.append(convolve(xc, ws, lambda v: v * spread_b, o_sg, 1))
+
     arrived(ag, 2, GROUP)
     for be in range(TAPS):
         v = ag[:, be, :]
@@ -323,31 +320,48 @@
         copy.wait()
 
 
+def deliver(pred, sg, kg, bias, o_pred, o_sg, o_kg, o_bias, sems):
+    copies = [
+        pltpu.make_async_copy(source, target, sems.at[i])
+        for i, (source, target) in enumerate(((pred, o_pred), (sg, o_sg), (kg, o_kg), (bias, o_bias)))
+    ]
+    for copy in copies:
+        copy.start()
+    for copy in copies:
+        copy.wait()
+
+
 def body(snapshot, snap_index, snap_means, snap_scales, out_bias, weights, cotangent):
     cells = PLANES * 4 * ROWS * 4 * LANES
     scale = 1.0 / math.sqrt(cells)
     shape = jax.ShapeDtypeStruct
     dma = pltpu.SemaphoreType.DMA
     vmem = pltpu.VMEM
-    hbm = pl.BlockSpec(memory_space=pl.ANY)
+    hbm = pl.BlockSpec(memory_space=pltpu.HBM)
+    anywhere = pl.BlockSpec(memory_space=pl.ANY)
     local = pl.BlockSpec(memory_space=pltpu.VMEM)
     tile = (C, LANES)
-    pred, sg, kg, bias = pl.pallas_call(
+    results = (
+        shape((C, ROWS, LANES), BF16),
+        shape((C, ROWS, LANES), BF16),
+        shape((27, C, C), F32),
+        shape((1, C), F32),
+    )
+    computed = pl.pallas_call(
         functools.partial(kernel, scale),
-        out_shape=(
-            shape((C, ROWS, LANES), BF16),
-            shape((C, ROWS, LANES), BF16),
-            shape((27, C, C), F32),
-            shape((1, C), F32),
-        ),
-        in_specs=[hbm, hbm, local, local, local, local, hbm],
-        out_specs=(hbm, hbm, local, local),
+        out_shape=results,
+        in_specs=[hbm] * 7,
+        out_specs=(anywhere, anywhere, local, local),
         scratch_shapes=[
             vmem((2, C, ROWS, LANES), BF16),
-            vmem((2, C, ROWS, LANES), BF16),
-            vmem((2, C, ROWS, LANES), BF16),
+            vmem((2, 2, C, HALF, LANES), BF16),
+            vmem((2, 2, C, HALF, LANES), BF16),
             vmem((27, C, C), BF16),
-            vmem((C * ROWS, LANES), F32),
+            vmem((1, 1), jnp.int32),
+            vmem((C, 64), F32),
+            vmem((C, 64), F32),
+            vmem((1, C), F32),
+            vmem((2, C * ROWS, LANES), F32),
             vmem((4 * C, BLOCKS * LANES), BF16),
             vmem((3 * C, BLOCKS * LANES), BF16),
             vmem((3 * C, BLOCKS * LANES), BF16),
@@ -360,7 +374,7 @@
             vmem((2, 3) + tile, BF16),
             vmem((2, 2, 3) + tile, BF16),
             vmem((TAPS * C, BLOCKS * LANES), F32),
-            vmem((C * ROWS, LANES), F32),
+            vmem((2, C * ROWS, LANES), F32),
             vmem((2, C, ROWS, LANES), BF16),
             vmem((TAPS * C, LANES), F32),
             vmem((GROUP, TAPS, LANES), F32),
@@ -368,9 +382,9 @@
             vmem((TAPS, LANES), F32),
             vmem((ZS, TAPS, LANES), F32),
             vmem((GROUP, TAPS, LANES), F32),
-            dma((3,)),
-            dma((2, 2)),
-            dma((2, 2)),
+            dma((7,)),
+            dma((2, 2, 2)),
+            dma((2, 2, 2)),
             dma((3, 3)),
             dma((3, 3)),
             dma((2,)),
@@ -380,7 +394,7 @@
             dma((2,)),
         ],
         compiler_params=pltpu.CompilerParams(
-            collective_id=0, has_side_effects=True, vmem_limit_bytes=32 * 2**20
+            collective_id=0, has_side_effects=True, vmem_limit_bytes=60 * 2**20
         ),
     )(
         snapshot.reshape(C, ROWS, LANES),
@@ -391,6 +405,13 @@
         out_bias.reshape(1, C),
         weights.transpose(2, 3, 4, 0, 1).reshape(27, C, C),
     )
+    pred, sg, kg, bias = pl.pallas_call(
+        deliver,
+        out_shape=results,
+        in_specs=[local] * 4,
+        out_specs=(hbm,) * 4,
+        scratch_shapes=[dma((4,))],
+    )(*computed)
     return (
         pred.reshape(C, 1, ROWS, LANES),
         sg.reshape(C, 1, ROWS, LANES),

time: 52.7 us -> 43.1 us (0.82)
  local copies, waits for them, and re-layouts: 7.6 us -> 0 us
  Pallas kernels: 43.5 us -> 41.4 us
    unnamed x16 -> x0, local copies, waits for them, and re-layouts: 7.6 us -> none
    pallas_call x1 -> x2, Pallas kernels: 43.5 us -> 41.4 us  [the longest x1 39.3 us: body(): pl.pallas_call(functools.partial(kernel, scale), out_shape=results, in_sp...]
where the time goes in v2:
time: 43.1 us; the launch traced here: 42.7 us
  Pallas kernels  41.4 us (96%)
  between operations  1.29 us (3%)
    pallas_call x1, Pallas kernels, body(): pl.pallas_call(functools.partial(kernel, scale), out_shape=results, in_sp...  39.3 us
    pallas_call x1, Pallas kernels, body(): pl.pallas_call(deliver, out_shape=results, in_specs=[local] * 4, out_spec...  2.15 us

profile of v2, /device:TPU:1, one launch (start us, length us, event | category | flops | bytes accessed | tf_op | source)
XLA Modules:
  0.0 42.7 jit_solution(1062545031585177673)
XLA Ops:
  1.3 39.3 %shard_map.102 = (bf16[32,32,128]{2,1,0:T(8,128)(2,1)}, bf16[32,32,128]{2,1,0:T(8,128)(2,1)}, f32[27,32,32]{2,1,0:T(8,128)}, f32[1,32]{1,0:T(1,128)}) custom-call(bf16[32,32,128]{2,1,0:T(8,128)(2,1)} %bitcast.20, bf16[32,32,128]{2,1,0:T(8,128)(2,1)} %bitcast.21, s32[1,1]{1,0:T(1,128)} %bitcast.19.idx_in, f32[32,64]{1,0:T(8,128)} %bitcast.23, ...), custom_call_target="tpu_custom_call" | custom-call | tf_op jit(solution)/shard_map/pallas_call | solution.py:350
  40.6 2.1 %shard_map.103 = (bf16[32,32,128]{2,1,0:T(8,128)(2,1)}, bf16[32,32,128]{2,1,0:T(8,128)(2,1)}, f32[27,32,32]{2,1,0:T(8,128)}, f32[1,32]{1,0:T(1,128)}) custom-call(bf16[32,32,128]{2,1,0:T(8,128)(2,1)} %get-tuple-element.12.pred, bf16[32,32,128]{2,1,0:T(8,128)(2,1)} %get-tuple-element.13.sg, f32[27,32,32]{2,1,0:T(8,128)} %get-tuple-element.14.kg, ...), custom_call_target="tpu_custom_call" | custom-call | tf_op jit(solution)/shard_map/pallas_call | solution.py:408

commit v3 on v2

--- a/solution.py
+++ b/solution.py
@@ -32,10 +32,10 @@
 def kernel(
     scale,
     snap, cot, idx_in, means_in, scales_in, bias_in, weights,
-    o_pred, o_sg, o_kg, o_bias,
+    o_pred, o_sg, o_sum,
     raw_own, raw_n, raw_c, w_raw, idx, means, scales, bias, flat, xn, xc, d, wp, ws,
     edge, side, edge_in, side_in, pack, pack_in,
-    res, out32, out16, kg_acc, kg_own, rs_in, z_own, z_in, ag,
+    res, out32, out16, kg_acc, kg_own, rs_in, z_own, z_in, total_own,
     s_load, s_bulk, r_bulk, s_halo, r_halo, s_pack, r_pack, s_sum, r_sum, s_out,
 ):
     gx, gy, gz = lax.axis_index("gx"), lax.axis_index("gy"), lax.axis_index("gz")
@@ -57,8 +57,7 @@
         pltpu.make_async_copy(scales_in, scales, s_load.at[5]),
         pltpu.make_async_copy(bias_in, bias, s_load.at[6]),
     ]
-    for copy in loads:
-        copy.start()
+    loads[0].start()
 
     next_x = [lax.rem(gx + 1, PLANES), lax.rem(gx + PLANES - 1, PLANES)]
     barrier = pltpu.get_barrier_semaphore()
@@ -87,6 +86,8 @@
     bulk_c = bulk(1, cot, raw_c)
     for copy in bulk_n:
         copy.start()
+    for i in (4, 5, 3, 1, 2, 6):
+        loads[i].start()
 
     for copy in loads[3:]:
         copy.wait()
@@ -295,8 +296,10 @@
     total = z_in[0]
     for k in range(1, ZS):
         total = total + z_in[k]
-    ag[me] = total * scale
-    spread_out(lambda p: ag.at[me], ag, me, 2, group_peers, member)
+    total_own[...] = total * scale
+    spread_out(lambda p: total_own, o_sum, me, 2, group_peers, member)
+    mine = pltpu.make_async_copy(total_own, o_sum.at[me], s_out.at[2])
+    mine.start()
     for copy in bulk_c:
         copy.wait()
     for way in range(2):
@@ -307,27 +310,39 @@
             )
     written.append(convolve(xc, ws, lambda v: v * spread_b, o_sg, 1))
 
-    arrived(ag, 2, GROUP)
+    arrived(o_sum, 2, GROUP)
+    mine.wait()
+    for copy in written:
+        copy.wait()
+
+
+def deliver(pred, sg, sums, o_pred, o_sg, o_kg, o_bias, pred_v, sg_v, sums_v, kg_v, bias_v, s_in, s_out):
+    arrivals = [
+        pltpu.make_async_copy(source, target, s_in.at[i])
+        for i, (source, target) in enumerate(((sums, sums_v), (pred, pred_v), (sg, sg_v)))
+    ]
+    for copy in arrivals:
+        copy.start()
+    departures = [
+        pltpu.make_async_copy(source, target, s_out.at[i])
+        for i, (source, target) in enumerate(((kg_v, o_kg), (pred_v, o_pred), (sg_v, o_sg), (bias_v, o_bias)))
+    ]
+    arrivals[0].wait()
     for be in range(TAPS):
-        v = ag[:, be, :]
+        v = sums_v[:, be, :]
         for a in range(3):
             turned = v if a == 0 else pltpu.roll(v, LANES - a * C, 1)
-            o_kg[a * TAPS + be] = turned[:, :C]
+            kg_v[a * TAPS + be] = turned[:, :C]
         if be == 4:
             column = jnp.broadcast_to(v[:, 3 * C : 3 * C + 1], (C, C))
-            o_bias[...] = jnp.sum(jnp.where(eye32, column, 0.0), 0, keepdims=True)
-    for copy in written:
-        copy.wait()
-
-
-def deliver(pred, sg, kg, bias, o_pred, o_sg, o_kg, o_bias, sems):
-    copies = [
-        pltpu.make_async_copy(source, target, sems.at[i])
-        for i, (source, target) in enumerate(((pred, o_pred), (sg, o_sg), (kg, o_kg), (bias, o_bias)))
-    ]
-    for copy in copies:
-        copy.start()
-    for copy in copies:
+            diagonal = lax.broadcasted_iota(jnp.int32, (C, C), 0) == lax.broadcasted_iota(jnp.int32, (C, C), 1)
+            bias_v[...] = jnp.sum(jnp.where(diagonal, column, 0.0), 0, keepdims=True)
+    departures[0].start()
+    departures[3].start()
+    for i in (1, 2):
+        arrivals[i].wait()
+        departures[i].start()
+    for copy in departures:
         copy.wait()
 
 
@@ -339,7 +354,6 @@
     vmem = pltpu.VMEM
     hbm = pl.BlockSpec(memory_space=pltpu.HBM)
     anywhere = pl.BlockSpec(memory_space=pl.ANY)
-    local = pl.BlockSpec(memory_space=pltpu.VMEM)
     tile = (C, LANES)
     results = (
         shape((C, ROWS, LANES), BF16),
@@ -349,9 +363,9 @@
     )
     computed = pl.pallas_call(
         functools.partial(kernel, scale),
-        out_shape=results,
+        out_shape=results[:2] + (shape((GROUP, TAPS, LANES), F32),),
         in_specs=[hbm] * 7,
-        out_specs=(anywhere, anywhere, local, local),
+        out_specs=(anywhere,) * 3,
         scratch_shapes=[
             vmem((2, C, ROWS, LANES), BF16),
             vmem((2, 2, C, HALF, LANES), BF16),
@@ -381,7 +395,7 @@
             vmem((GROUP, TAPS, LANES), F32),
             vmem((TAPS, LANES), F32),
             vmem((ZS, TAPS, LANES), F32),
-            vmem((GROUP, TAPS, LANES), F32),
+            vmem((TAPS, LANES), F32),
             dma((7,)),
             dma((2, 2, 2)),
             dma((2, 2, 2)),
@@ -391,7 +405,7 @@
             dma((2,)),
             dma((3,)),
             dma((3,)),
-            dma((2,)),
+            dma((3,)),
         ],
         compiler_params=pltpu.CompilerParams(
             collective_id=0, has_side_effects=True, vmem_limit_bytes=60 * 2**20
@@ -408,9 +422,18 @@
     pred, sg, kg, bias = pl.pallas_call(
         deliver,
         out_shape=results,
-        in_specs=[local] * 4,
+        in_specs=[anywhere] * 3,
         out_specs=(hbm,) * 4,
-        scratch_shapes=[dma((4,))],
+        scratch_shapes=[
+            vmem((C, ROWS, LANES), BF16),
+            vmem((C, ROWS, LANES), BF16),
+            vmem((GROUP, TAPS, LANES), F32),
+            vmem((27, C, C), F32),
+            vmem((1, C), F32),
+            dma((3,)),
+            dma((4,)),
+        ],
+        compiler_params=pltpu.CompilerParams(vmem_limit_bytes=60 * 2**20),
     )(*computed)
     return (
         pred.reshape(C, 1, ROWS, LANES),

time: 43.1 us -> 40.5 us (0.940)
  Pallas kernels: 41.4 us -> 39.1 us
    pallas_call x2, Pallas kernels: 41.4 us -> 39.1 us  [the longest x1 37 us: body(): pl.pallas_call(functools.partial(kernel, scale), out_shape=results[:2] +...]
where the time goes in v3:
time: 40.5 us; the launch traced here: 40.3 us
  Pallas kernels  39.1 us (97%)
  between operations  1.29 us (3%)
    pallas_call x1, Pallas kernels, body(): pl.pallas_call(functools.partial(kernel, scale), out_shape=results[:2] +...  37 us
    pallas_call x1, Pallas kernels, body(): pl.pallas_call(deliver, out_shape=results, in_specs=[anywhere] * 3, out_s...  2.1 us

profile of v3, /device:TPU:1, one launch (start us, length us, event | category | flops | bytes accessed | tf_op | source)
XLA Modules:
  0.0 40.3 jit_solution(15019694891166463518)
XLA Ops:
  1.3 37.0 %shard_map.102 = (bf16[32,32,128]{2,1,0:T(8,128)(2,1)}, bf16[32,32,128]{2,1,0:T(8,128)(2,1)}, f32[32,9,128]{2,1,0:T(8,128)}) custom-call(bf16[32,32,128]{2,1,0:T(8,128)(2,1)} %bitcast.20, bf16[32,32,128]{2,1,0:T(8,128)(2,1)} %bitcast.21, s32[1,1]{1,0:T(1,128)} %bitcast.19.idx_in, f32[32,64]{1,0:T(8,128)} %bitcast.23, f32[32,64]{1,0:T(8,128)} %bitcast.24, ...), custom_call_target="tpu_custom_call" | custom-call | tf_op jit(solution)/shard_map/pallas_call | solution.py:364
  38.2 2.1 %shard_map.103 = (bf16[32,32,128]{2,1,0:T(8,128)(2,1)}, bf16[32,32,128]{2,1,0:T(8,128)(2,1)}, f32[27,32,32]{2,1,0:T(8,128)}, f32[1,32]{1,0:T(1,128)}) custom-call(bf16[32,32,128]{2,1,0:T(8,128)(2,1)} %get-tuple-element.11.pred, bf16[32,32,128]{2,1,0:T(8,128)(2,1)} %get-tuple-element.12.sg, f32[32,9,128]{2,1,0:T(8,128)} %get-tuple-element.13.sums), custom_call_target="tpu_custom_call" | custom-call | tf_op jit(solution)/shard_map/pallas_call | solution.py:422

commit v4 on v3

--- a/solution.py
+++ b/solution.py
@@ -245,42 +245,33 @@
         copy.start()
     rs_in[me] = kg_own[me]
 
-    def convolve(x, filters, finish, target, field):
-        res[...] = jnp.dot(filters[...], x[pl.ds(0, 3 * C), :], preferred_element_type=F32)
-
-        def of(b, e):
-            return pl.ds((b * 3 + e) * C, C)
-
+    def of(b, e):
+        return pl.ds((b * 3 + e) * C, C)
+
+    def multiply(x, filters, first, count):
+        at = pl.ds(first * LANES, count * LANES)
+        res[:, at] = jnp.dot(filters[...], x[pl.ds(0, 3 * C), at], preferred_element_type=F32)
+
+    def add_up(finish, field, first, last):
         left = res[of(0, 0), block(HALO)]
         right = res[of(0, 2), block(HALO)]
         for b in range(1, 3):
             left = left + pltpu.roll(res[of(b, 0), block(HALO)], LANES - b, 1)
             right = right + pltpu.roll(res[of(b, 2), block(HALO)], LANES - b, 1)
-
-        for y in range(ROWS):
+        for y in range(first, last):
             s = [sum(res[of(b, e), block(y + b)] for b in range(3)) for e in range(3)]
             from_left = jnp.where(lane == 0, pltpu.roll(left, (LANES - y) % LANES, 1), pltpu.roll(s[0], 1, 1))
             from_right = jnp.where(
                 lane == LANES - 1, pltpu.roll(right, LANES - 1 - RIGHT - y, 1), pltpu.roll(s[2], LANES - 1, 1)
             )
             out32[field, pl.ds(y, C, stride=ROWS), :] = finish(s[1] + from_left + from_right)
+
+    def write(target, field):
         for c in range(0, C, 8):
             out16[field, pl.ds(c, 8)] = out32[field, pl.ds(c * ROWS, 8 * ROWS), :].reshape(8, ROWS, LANES).astype(BF16)
         copy = pltpu.make_async_copy(out16.at[field], target, s_out.at[field])
         copy.start()
         return copy
-
-    for copy in packs:
-        copy.wait()
-    for way in range(2):
-        for f in range(2):
-            for i, b in enumerate((TOP, BOTTOM, HALO)):
-                fields[f][pl.ds(way * 2 * C, C), block(b)] = pack_in[way, f, i]
-
-    eye32 = lax.broadcasted_iota(jnp.int32, (C, C), 0) == lax.broadcasted_iota(jnp.int32, (C, C), 1)
-    bias_col = jnp.sum(jnp.where(eye32, jnp.broadcast_to(bias[...], (C, C)), 0.0), 1, keepdims=True)
-    bias_b = jnp.broadcast_to(bias_col, (C, LANES))
-    written = [convolve(xn, wp, lambda v: v + bias_b, o_pred, 0)]
 
     arrived(rs_in, 0, GROUP)
     total = rs_in[0]
@@ -300,16 +291,41 @@
     spread_out(lambda p: total_own, o_sum, me, 2, group_peers, member)
     mine = pltpu.make_async_copy(total_own, o_sum.at[me], s_out.at[2])
     mine.start()
-    for copy in bulk_c:
+    for copy in packs:
         copy.wait()
     for way in range(2):
-        for half in range(2):
-            relayout(
-                raw_c.at[way, half], flat.at[way, pl.ds(half * C * HALF, C * HALF)],
-                xc, way * 2 * C, half * HALF, HALF, False, False,
-            )
-    written.append(convolve(xc, ws, lambda v: v * spread_b, o_sg, 1))
-
+        for f in range(2):
+            for i, b in enumerate((TOP, BOTTOM, HALO)):
+                fields[f][pl.ds(way * 2 * C, C), block(b)] = pack_in[way, f, i]
+
+    eye32 = lax.broadcasted_iota(jnp.int32, (C, C), 0) == lax.broadcasted_iota(jnp.int32, (C, C), 1)
+    bias_col = jnp.sum(jnp.where(eye32, jnp.broadcast_to(bias[...], (C, C)), 0.0), 1, keepdims=True)
+    bias_b = jnp.broadcast_to(bias_col, (C, LANES))
+    multiply(xn, wp, 0, BLOCKS)
+    add_up(lambda v: v + bias_b, 0, 0, ROWS)
+    written = [write(o_pred, 0)]
+
+    for copy in bulk_c[:2]:
+        copy.wait()
+    for way in range(2):
+        relayout(
+            raw_c.at[way, 0], flat.at[way, pl.ds(0, C * HALF)],
+            xc, way * 2 * C, 0, HALF, False, False,
+        )
+    multiply(xc, ws, 0, HALF + 1)
+    multiply(xc, ws, HALO, 1)
+    add_up(lambda v: v * spread_b, 1, 0, HALF - 1)
+
+    for copy in bulk_c[2:]:
+        copy.wait()
+    for way in range(2):
+        relayout(
+            raw_c.at[way, 1], flat.at[way, pl.ds(C * HALF, C * HALF)],
+            xc, way * 2 * C, HALF, HALF, False, False,
+        )
+    multiply(xc, ws, HALF + 1, HALF + 1)
+    add_up(lambda v: v * spread_b, 1, HALF - 1, ROWS)
+    written.append(write(o_sg, 1))
     arrived(o_sum, 2, GROUP)
     mine.wait()
     for copy in written:

time: 40.5 us -> 39.8 us (0.983)
  Pallas kernels: 39.1 us -> 38.4 us
    pallas_call x1, Pallas kernels: 37 us -> 36.3 us  [body(): pl.pallas_call(functools.partial(kernel, scale), out_shape=results[:2] +...]
where the time goes in v4:
time: 39.8 us; the launch traced here: 39.7 us
  Pallas kernels  38.4 us (96%)
  between operations  1.29 us (3%)
    pallas_call x1, Pallas kernels, body(): pl.pallas_call(functools.partial(kernel, scale), out_shape=results[:2] +...  36.3 us
    pallas_call x1, Pallas kernels, body(): pl.pallas_call(deliver, out_shape=results, in_specs=[anywhere] * 3, out_s...  2.1 us

profile of v4, /device:TPU:1, one launch (start us, length us, event | category | flops | bytes accessed | tf_op | source)
XLA Modules:
  0.0 39.7 jit_solution(3761030072377664219)
XLA Ops:
  1.3 36.3 %shard_map.102 = (bf16[32,32,128]{2,1,0:T(8,128)(2,1)}, bf16[32,32,128]{2,1,0:T(8,128)(2,1)}, f32[32,9,128]{2,1,0:T(8,128)}) custom-call(bf16[32,32,128]{2,1,0:T(8,128)(2,1)} %bitcast.20, bf16[32,32,128]{2,1,0:T(8,128)(2,1)} %bitcast.21, s32[1,1]{1,0:T(1,128)} %bitcast.19.idx_in, f32[32,64]{1,0:T(8,128)} %bitcast.23, f32[32,64]{1,0:T(8,128)} %bitcast.24, ...), custom_call_target="tpu_custom_call" | custom-call | tf_op jit(solution)/shard_map/pallas_call | solution.py:380
  37.6 2.1 %shard_map.103 = (bf16[32,32,128]{2,1,0:T(8,128)(2,1)}, bf16[32,32,128]{2,1,0:T(8,128)(2,1)}, f32[27,32,32]{2,1,0:T(8,128)}, f32[1,32]{1,0:T(1,128)}) custom-call(bf16[32,32,128]{2,1,0:T(8,128)(2,1)} %get-tuple-element.11.pred, bf16[32,32,128]{2,1,0:T(8,128)(2,1)} %get-tuple-element.12.sg, f32[32,9,128]{2,1,0:T(8,128)} %get-tuple-element.13.sums), custom_call_target="tpu_custom_call" | custom-call | tf_op jit(solution)/shard_map/pallas_call | solution.py:438

commit v5 on v4

--- a/solution.py
+++ b/solution.py
@@ -202,7 +202,7 @@
     total = None
     for half in range(2):
         for way in range(2):
-            bulk_n[2 * half + way].wait()
+            bulk_n[2 * half + way].wait_recv()
         for way in range(2):
             relayout(
                 raw_n.at[way, half], flat.at[way, pl.ds(half * C * HALF, C * HALF)],
@@ -214,10 +214,8 @@
         part = lax.dot_general(left, right, (((1,), (1,)), ((), ())), preferred_element_type=F32)
         if half == 0:
             kg_acc[...] = part
-        else:
-            kg_acc[...] += part
     for be in range(TAPS):
-        kg_own[:, be, :] = kg_acc[pl.ds(be * C, C), :]
+        kg_own[:, be, :] = kg_acc[pl.ds(be * C, C), :] + part[be * C : (be + 1) * C]
 
     near = {0: 0, 1: 1, 2: 2, 3: 1}
     steps = [(dy, dc, dx) for dy in range(4) for dc in range(2) for dx in range(4)][1:]
@@ -238,6 +236,9 @@
     def arrived(landing, stage, count):
         all_of = landing.at[pl.ds(0, count - 1)]
         pltpu.make_async_copy(all_of, all_of, r_sum.at[stage]).wait()
+
+    def sent(landing, stage, count):
+        all_of = landing.at[pl.ds(0, count - 1)]
         pltpu.make_async_copy(all_of, all_of, s_sum.at[stage]).wait()
 
     spread_out(lambda p: kg_own.at[p], rs_in, me, 0, group_peers, member)
@@ -326,6 +327,11 @@
     multiply(xc, ws, HALF + 1, HALF + 1)
     add_up(lambda v: v * spread_b, 1, HALF - 1, ROWS)
     written.append(write(o_sg, 1))
+    for copy in bulk_n:
+        copy.wait_send()
+    stages = ((rs_in, 0, GROUP), (z_in, 1, ZS), (o_sum, 2, GROUP))
+    for landing, stage, count in stages:
+        sent(landing, stage, count)
     arrived(o_sum, 2, GROUP)
     mine.wait()
     for copy in written:

time: 39.8 us -> 39.8 us (level)
  no operation moved by 1% of the time
where the time goes in v5:
time: 39.8 us; the launch traced here: 39.6 us
  Pallas kernels  38.3 us (96%)
  between operations  1.29 us (3%)
    pallas_call x1, Pallas kernels, body(): pl.pallas_call(functools.partial(kernel, scale), out_shape=results[:2] +...  36.2 us
    pallas_call x1, Pallas kernels, body(): pl.pallas_call(deliver, out_shape=results, in_specs=[anywhere] * 3, out_s...  2.1 us

profile of v5, /device:TPU:1, one launch (start us, length us, event | category | flops | bytes accessed | tf_op | source)
XLA Modules:
  0.0 39.6 jit_solution(11565304348816586766)
XLA Ops:
  1.3 36.2 %shard_map.102 = (bf16[32,32,128]{2,1,0:T(8,128)(2,1)}, bf16[32,32,128]{2,1,0:T(8,128)(2,1)}, f32[32,9,128]{2,1,0:T(8,128)}) custom-call(bf16[32,32,128]{2,1,0:T(8,128)(2,1)} %bitcast.20, bf16[32,32,128]{2,1,0:T(8,128)(2,1)} %bitcast.21, s32[1,1]{1,0:T(1,128)} %bitcast.19.idx_in, f32[32,64]{1,0:T(8,128)} %bitcast.23, f32[32,64]{1,0:T(8,128)} %bitcast.24, ...), custom_call_target="tpu_custom_call" | custom-call | tf_op jit(solution)/shard_map/pallas_call | solution.py:386
  37.5 2.1 %shard_map.103 = (bf16[32,32,128]{2,1,0:T(8,128)(2,1)}, bf16[32,32,128]{2,1,0:T(8,128)(2,1)}, f32[27,32,32]{2,1,0:T(8,128)}, f32[1,32]{1,0:T(1,128)}) custom-call(bf16[32,32,128]{2,1,0:T(8,128)(2,1)} %get-tuple-element.11.pred, bf16[32,32,128]{2,1,0:T(8,128)(2,1)} %get-tuple-element.12.sg, f32[32,9,128]{2,1,0:T(8,128)} %get-tuple-element.13.sums), custom_call_target="tpu_custom_call" | custom-call | tf_op jit(solution)/shard_map/pallas_call | solution.py:444
